TPU v7x, 256 devices: a whole 4x4x8 slice. The times are simulated.
256 devices in a mesh: theta: 32 (over z, y_lo, core), row: 8 (over y_hi, x).
Axes of the slice: x: 4, y: 4 (y_hi: 2, y_lo: 2; y = y_hi * 2 + y_lo), z: 8, core: 2. Of those that a mesh axis runs over, the one named last changes fastest.
Arguments:
- rhs: float32 [5, 32, 256, 4096], P(None, None, 'row', 'theta'), may hold values from -8 to 8
- decay_radial: float32 [2, 5, 32], replicated, may hold values from 1 to 170
- decay_theta: float32 [2, 5, 32], replicated, may hold values from 1 to 2730
- mix_mid: float32 [5, 5, 32, 256], P(None, None, None, 'row'), may hold values from -2 to 3
- mix_out: float32 [5, 5, 32, 256], P(None, None, None, 'row'), may hold values from -2 to 3
Outputs:
- update: float32 [5, 32, 256, 4096], P(None, None, 'row', 'theta')
All inputs are finite; a program needn't handle non-finite values.
Results may differ from a plain program's by a relative error of at most 0.0003.
Values sent between devices are 32-bit elements; how exact they have to be, the bound alone decides.
A program may use at most 192 MiB of HBM per device.

v0:
```python
import functools

import jax
import jax.numpy as jnp
from jax import lax
from jax.experimental import pallas as pl
from jax.experimental.pallas import tpu as pltpu
from jax.sharding import PartitionSpec as P

MESH = pl.DeviceIdType.MESH
KC = 8
SLOT = 24
F32 = jnp.float32
BF16 = jnp.bfloat16


def gap(u):
    h = 0.5 * u
    q = h * h
    series = 1.0 + q / 6.0 * (1.0 + q / 20.0 * (1.0 + q / 42.0 * (1.0 + q / 72.0)))
    return 2.0 * jnp.exp(-h) * h * series


def split(x):
    hi = x.astype(BF16)
    return hi, (x - hi.astype(F32)).astype(BF16)


def block_transfer(u1, u2, doublings):
    a, b = jnp.exp(-u1), jnp.exp(-u2)
    c = a
    q11, q12, q21, q22 = a, b, a, b
    for _ in range(doublings):
        x11, x12 = q11 * a + q12 * c, q12 * b
        x21, x22 = q21 * a + q22 * c, q22 * b
        q11, q12, q21, q22 = (
            q11 + a * x11,
            q12 + a * x12,
            q21 + c * x11 + b * x21,
            q22 + c * x12 + b * x22,
        )
        c = c * (a + b)
        a, b = a * a, b * b
    return a, b, c, q11, q12, q21, q22


def pick_lane(values, index):
    lane = lax.broadcasted_iota(jnp.int32, values.shape, 1)
    return jnp.sum(jnp.where(lane == index, values, 0.0), axis=1, keepdims=True)


def power_tables(u1, u2, n, bits):
    nf = n.astype(F32)
    a, b = jnp.exp(-nf * u1), jnp.exp(-nf * u2)
    ab, bb = jnp.exp(-u1), jnp.exp(-u2)
    pb = jnp.ones_like(ab)
    p = jnp.zeros_like(nf * u1)
    low = jnp.ones_like(p)
    for bit in range(bits):
        has = (n >> bit) & 1 == 1
        p = jnp.where(has, ab * p + low * pb, p)
        low = jnp.where(has, low * bb, low)
        pb = pb * (ab + bb)
        ab, bb = ab * ab, bb * bb
    return a, b, p


def solve_kernel(
    sizes, rhs, dr, dt, mixm, mixo, l2_out, infl_out, etab,
    xin, xm, zbuf, l2buf, ybuf, rcoef, mcoef, gtab, wtab, xhi, xlo,
    e1, rcv1, o1, rcv2, tx1, trc1, tx2, trc2,
    in_sem, s1s, s1r, s2s, s2r, t1s, t1r, t2s, t2r, out_sem, fin_sem,
):
    V, K, RL, TL, nrow, nth = sizes
    nchunk = K // KC
    me_r = lax.axis_index("row")
    me_t = lax.axis_index("theta")
    kr = KC * RL

    def in_copy(c):
        return pltpu.make_async_copy(rhs.at[:, pl.ds(c * kr, kr), :], xin.at[c], in_sem.at[c])

    for c in range(nchunk):
        in_copy(c).start()

    barrier = pltpu.get_barrier_semaphore()

    @pl.loop(1, nrow)
    def _(d):
        pl.semaphore_signal(barrier, inc=1, device_id={"row": lax.rem(me_r + d, nrow)}, device_id_type=MESH)

    @pl.loop(1, nth)
    def _(d):
        pl.semaphore_signal(barrier, inc=1, device_id={"theta": lax.rem(me_t + d, nth)}, device_id_type=MESH)

    cells_r = RL * nrow
    ur1, ur2 = dr[0] / cells_r, dr[1] / cells_r
    fr = gap(ur1) * gap(ur2)
    diag = lax.broadcasted_iota(jnp.int32, (K, K), 0) == lax.broadcasted_iota(jnp.int32, (K, K), 1)
    for j, table in enumerate((jnp.exp(-ur1), jnp.exp(-ur2), fr * fr)):
        for m in range(V):
            column = jnp.sum(
                jnp.where(diag, jnp.broadcast_to(table[m : m + 1, :], (K, K)), 0.0), axis=1, keepdims=True
            )
            rcoef[j, m] = jnp.broadcast_to(column, (K, TL))
    radial_block = block_transfer(ur1, ur2, RL.bit_length() - 1)

    def radial_pass(c, states, emit):
        r1 = [rcoef[0, m, pl.ds(c * KC, KC), :] for m in range(V)]
        r2 = [rcoef[1, m, pl.ds(c * KC, KC), :] for m in range(V)]

        def ahead(r, carry):
            out = []
            for m in range(V):
                s1, s2 = carry[m]
                s1 = r1[m] * s1 + xin[c, m, pl.ds(r, KC, stride=RL), :]
                s2 = r2[m] * s2 + s1
                ybuf[m, pl.ds(pl.multiple_of(r * KC, KC), KC), :] = s2
                out.append((s1, s2))
            return tuple(out)

        def behind(i, carry):
            r = RL - 1 - i
            out = []
            for m in range(V):
                u1, u2 = carry[m]
                u1 = r1[m] * u1 + ybuf[m, pl.ds(pl.multiple_of(r * KC, KC), KC), :]
                u2 = r2[m] * u2 + u1
                out.append((u1, u2))
            if emit is not None:
                emit(r, [pair[1] for pair in out])
            return tuple(out)

        first = lax.fori_loop(0, RL, ahead, tuple((s[0], s[1]) for s in states), unroll=4)
        second = lax.fori_loop(0, RL, behind, tuple((s[2], s[3]) for s in states), unroll=4)
        return first, second

    @pl.loop(0, nchunk)
    def _(c):
        in_copy(c).wait()
        zero = jnp.zeros((KC, TL), F32)
        first, second = radial_pass(c, [(zero,) * 4] * V, None)
        for m in range(V):
            for s, value in enumerate((first[m][0], first[m][1], second[m][0], second[m][1])):
                e1[c, pl.ds(s * V + m, KC, stride=SLOT), :] = value

        @pl.when(c == 0)
        def _():
            pl.semaphore_wait(barrier, nrow - 1 + nth - 1)

        @pl.loop(1, nrow)
        def _(d):
            p = lax.rem(me_r + d, nrow)
            pltpu.make_async_remote_copy(
                src_ref=e1.at[c, pl.ds(pl.multiple_of(p * SLOT, 8), SLOT), :],
                dst_ref=rcv1.at[c, me_r],
                send_sem=s1s.at[c],
                recv_sem=s1r.at[c],
                device_id={"row": p},
                device_id_type=MESH,
            ).start()

        pltpu.make_async_copy(
            e1.at[c, pl.ds(pl.multiple_of(me_r * SLOT, 8), SLOT), :], rcv1.at[c, me_r], s1r.at[c]
        ).start()

    cells_t = TL * nth
    ut1, ut2 = dt[0] / cells_t, dt[1] / cells_t
    lane = lax.broadcasted_iota(jnp.int32, (V, TL), 1)
    sub8 = lax.broadcasted_iota(jnp.int32, (8, TL), 0)
    lane8 = lax.broadcasted_iota(jnp.int32, (8, TL), 1)
    bits = TL.bit_length() - 1

    etab[...] = jnp.zeros_like(etab)
    wtab[...] = jnp.zeros_like(wtab)

    @pl.loop(0, K)
    def _(k):
        u1 = pick_lane(ut1, k)
        u2 = pick_lane(ut2, k)
        r1, r2 = jnp.exp(-u1), jnp.exp(-u2)
        f = gap(u1) * gap(u2)
        g12, g11, g22 = gap(u1 + u2), gap(2.0 * u1), gap(2.0 * u2)
        scale_1 = f * f * r1 / g12
        coef_a = scale_1 * (r1 / (g11 * g12) + r2 / (g12 * g22))
        coef_p = scale_1 / g22
        coef_b = f * f / (g12 * g22)
        af, bf, pf = power_tables(u1, u2, lane, bits)
        ar, br, pr = power_tables(u1, u2, TL - 1 - lane, bits)
        pf1, pr1 = r1 * pf + bf, r1 * pr + br
        h0 = coef_a * af + coef_p * pf + coef_b * bf
        e_s1 = coef_a * (r1 * af) + coef_p * pf1
        e_s2 = coef_b * (r2 * bf)
        e_t1 = coef_a * (r1 * ar) + coef_p * pr1
        e_t2 = coef_b * (r2 * br)
        h1 = e_t1 + e_t2
        for s, value in enumerate((e_s1, e_s2, e_t1, e_t2)):
            etab[k, 8 * s : 8 * s + V, :] = value
        for s, value in enumerate((ar, pr1, af, pf1)):
            hi, lo = split(value)
            wtab[k, 8 * s : 8 * s + V, :] = value
        for m in range(V):
            near = pltpu.roll(jnp.broadcast_to(h0[m : m + 1, :], (8, TL)), 0, 1, stride=1, stride_axis=0)
            far = pltpu.roll(jnp.broadcast_to(h1[m : m + 1, :], (8, TL)), 0, 1, stride=1, stride_axis=0)
            for b in range(TL // 16):
                rows = []
                for half in (0, 8):
                    shift = 16 * b + half
                    if shift:
                        left, right = pltpu.roll(far, shift, 1), pltpu.roll(near, shift, 1)
                    else:
                        left, right = far, near
                    rows.append(jnp.where(lane8 < shift + sub8, left, right))
                hi, lo = split(jnp.concatenate(rows, axis=0))
                gtab[k, m, 16 * b : 16 * b + 16, 0:TL] = hi
                gtab[k, m, 16 * b : 16 * b + 16, TL : 2 * TL] = lo

    def spread(which, table):
        @pl.loop(0, V * V)
        def _(q):
            @pl.loop(0, nchunk)
            def _(c):
                block = table[q, pl.ds(pl.multiple_of(c * KC, KC), KC), :]
                for r in range(RL):
                    mcoef[which, c, r, q] = jnp.broadcast_to(block[:, r : r + 1], (KC, TL))

    spread(0, mixm)

    @pl.loop(0, nchunk)
    def _(c):
        a, b, cc, q11, q12, q21, q22 = (
            jnp.broadcast_to(pick_lane(x, c * KC + me_r), (V, TL)) for x in radial_block
        )
        pltpu.make_async_copy(rcv1.at[c], rcv1.at[c], s1r.at[c]).wait()

        def got(d, s):
            return rcv1[c, d, s * V : s * V + V, :]

        zero = jnp.zeros((V, TL), F32)
        sa, sb = [zero], [zero]
        for d in range(nrow - 1):
            sa.append(a * sa[d] + got(d, 0))
            sb.append(b * sb[d] + cc * sa[d] + got(d, 1))
        ta, tb = zero, zero
        for d in range(nrow - 1, -1, -1):
            for s, value in enumerate((sa[d], sb[d], ta, tb)):
                o1[c, d, s * V : s * V + V, :] = value
            if d:
                ta, tb = (
                    a * ta + got(d, 2) + q11 * sa[d] + q12 * sb[d],
                    b * tb + cc * ta + got(d, 3) + q21 * sa[d] + q22 * sb[d],
                )

        @pl.loop(1, nrow)
        def _(i):
            p = lax.rem(me_r + i, nrow)
            pltpu.make_async_remote_copy(
                src_ref=o1.at[c, p],
                dst_ref=rcv2.at[c, pl.ds(pl.multiple_of(me_r * SLOT, 8), SLOT), :],
                send_sem=s2s.at[c],
                recv_sem=s2r.at[c],
                device_id={"row": p},
                device_id_type=MESH,
            ).start()

        pltpu.make_async_copy(
            o1.at[c, me_r], rcv2.at[c, pl.ds(pl.multiple_of(me_r * SLOT, 8), SLOT), :], s2r.at[c]
        ).start()

    spread(1, mixo)

    @pl.loop(0, nchunk)
    def _(c):
        pltpu.make_async_copy(rcv2.at[c], rcv2.at[c], s2r.at[c]).wait()
        states = [
            tuple(rcv2[c, pl.ds(s * V + m, KC, stride=SLOT), :] for s in range(4)) for m in range(V)
        ]
        f2 = [rcoef[2, m, pl.ds(c * KC, KC), :] for m in range(V)]

        def emit(r, z):
            z = [f2[m] * z[m] for m in range(V)]
            for m in range(V):
                total = mcoef[0, c, r, m * V] * z[0]
                for n in range(1, V):
                    total = total + mcoef[0, c, r, m * V + n] * z[n]
                xm[m, pl.ds(r, KC, stride=RL), :] = total

        radial_pass(c, states, emit)

        @pl.loop(0, KC)
        def _(kk):
            k = c * KC + kk
            rows = pl.ds(pl.multiple_of(kk * RL, RL), RL)
            hi, lo = split(jnp.concatenate([xm[m, rows, :] for m in range(V)], axis=0))
            xhi[k] = hi
            xlo[k] = lo
            whi, wlo = split(wtab[k])
            dims = (((1,), (1,)), ((), ()))
            out = lax.dot_general(jnp.concatenate([whi, wlo], axis=0), hi, dims, preferred_element_type=F32)
            out = out[0:32] + out[32:64] + lax.dot_general(whi, lo, dims, preferred_element_type=F32)
            both = []
            for s in range(4):
                first = out[8 * s : 8 * s + 8, 0:TL]
                last = jnp.concatenate([out[8 * s : 8 * s + 8, TL : TL + RL]] * 4, axis=1)
                both.append(jnp.where(sub8 == V - 1, last, first))
            message = jnp.zeros((8, TL), F32)
            for j in range(4):
                picked = both[(j + 3) % 4]
                for q in range(3):
                    picked = jnp.where(sub8 % 4 == q, both[(j + q) % 4], picked)
                moved = pltpu.roll(picked, j * RL, 1) if j else picked
                message = jnp.where(lane8 // RL == (sub8 + j) % 4, moved, message)
            tx1[k] = message[0:V]

            @pl.when(k == me_t)
            def _():
                pltpu.make_async_copy(tx1.at[k], trc1.at[me_t], t1r).start()

            @pl.when(k != me_t)
            def _():
                pltpu.make_async_remote_copy(
                    src_ref=tx1.at[k],
                    dst_ref=trc1.at[me_t],
                    send_sem=t1s,
                    recv_sem=t1r,
                    device_id={"theta": k},
                    device_id_type=MESH,
                ).start()

    def out_copy(c):
        return pltpu.make_async_copy(l2buf.at[c], l2_out.at[:, pl.ds(c * kr, kr), :], out_sem.at[c])

    def local_solve(c):
        @pl.loop(0, KC)
        def _(kk):
            k = c * KC + kk
            for m in range(V):
                hi = xhi[k, m * RL : m * RL + RL, :]
                lo = xlo[k, m * RL : m * RL + RL, :]
                ghi = gtab[k, m, :, 0:TL]
                glo = gtab[k, m, :, TL : 2 * TL]
                z = jnp.dot(jnp.concatenate([hi, lo], axis=0), ghi, preferred_element_type=F32)
                z = z[0:RL] + z[RL : 2 * RL] + jnp.dot(hi, glo, preferred_element_type=F32)
                zbuf[m, pl.ds(pl.multiple_of(kk * RL, RL), RL), :] = z

        def mix(r, carry):
            z = [zbuf[n, pl.ds(r, KC, stride=RL), :] for n in range(V)]
            for m in range(V):
                total = mcoef[1, c, r, m * V] * z[0]
                for n in range(1, V):
                    total = total + mcoef[1, c, r, m * V + n] * z[n]
                l2buf[c, m, pl.ds(r, KC, stride=RL), :] = total
            return carry

        lax.fori_loop(0, RL, mix, 0, unroll=4)
        out_copy(c).start()

    local_solve(0)

    u1, u2 = pick_lane(ut1, me_t), pick_lane(ut2, me_t)
    a, b, cc = (jnp.broadcast_to(x, (V, TL)) for x in block_transfer(u1, u2, bits)[:3])
    u1, u2 = jnp.broadcast_to(u1, (V, TL)), jnp.broadcast_to(u2, (V, TL))
    around_1 = 1.0 / (1.0 - jnp.exp(-cells_t * u1))
    around_2 = 1.0 / (1.0 - jnp.exp(-cells_t * u2))
    pltpu.make_async_copy(trc1, trc1, t1r).wait()
    forward = lane < 2 * RL
    entering = [jnp.where(forward, trc1[i], trc1[nth - 1 - i]) for i in range(nth)]

    def cycle(rate, decay, around, terms):
        chain = [jnp.zeros((V, TL), F32)]
        for i in range(nth):
            chain.append(rate * chain[i] + terms[i])
        start = chain[nth] * around
        return [chain[i] + jnp.exp(-(TL * i) * decay) * start for i in range(nth)]

    one = cycle(a, u1, around_1, entering)
    two = cycle(b, u2, around_2, [entering[i] + cc * pltpu.roll(one[i], RL, 1) for i in range(nth)])
    even = (lane // RL) % 2 == 0
    state = [jnp.where(even, one[i], two[i]) for i in range(nth)]
    for d in range(nth):
        tx2[d] = jnp.where(forward, state[d], state[nth - 1 - d])

    @pl.loop(1, nth)
    def _(i):
        d = lax.rem(me_t + i, nth)
        pltpu.make_async_remote_copy(
            src_ref=tx2.at[d],
            dst_ref=trc2.at[me_t],
            send_sem=t2s,
            recv_sem=t2r,
            device_id={"theta": d},
            device_id_type=MESH,
        ).start()

    pltpu.make_async_copy(tx2.at[me_t], trc2.at[me_t], t2r).start()

    @pl.loop(1, nchunk)
    def _(c):
        local_solve(c)

    pltpu.make_async_copy(trc2, trc2, t2r).wait()
    final = pltpu.make_async_copy(trc2, infl_out, fin_sem)
    final.start()

    @pl.loop(0, nchunk)
    def _(c):
        sent = rcv1.at[c, pl.ds(0, nrow - 1)]
        pltpu.make_async_copy(sent, sent, s1s.at[c]).wait()
        pltpu.make_async_copy(sent, sent, s2s.at[c]).wait()
        out_copy(c).wait()

    sent = trc1.at[pl.ds(0, nth - 1)]
    pltpu.make_async_copy(sent, sent, t1s).wait()
    pltpu.make_async_copy(sent, sent, t2s).wait()
    final.wait()


def finish_kernel(sizes, l2, infl, etab, mixo, out):
    V, K, RL, TL, nrow, nth = sizes
    kb = infl.shape[0]
    dims = (((0,), (0,)), ((), ()))
    for k in range(kb):
        inflow = infl[k]
        states = [inflow[:, s * RL : s * RL + RL] for s in range(4)]
        pad = jnp.zeros((8 - V, RL), F32)
        ehi, elo = split(etab[k])
        weights = jnp.concatenate([ehi, ehi, elo], axis=0)
        for m in range(V):
            gain = jnp.concatenate([mixo[m * V + n, k : k + 1, :] for n in range(V)], axis=0)
            parts = []
            for s in range(4):
                parts += [states[s] * gain, pad]
            hi, lo = split(jnp.concatenate(parts, axis=0))
            left = jnp.concatenate([hi, lo, hi], axis=0)
            rows = slice(k * RL, k * RL + RL)
            out[m, rows, :] = l2[m, rows, :] + lax.dot_general(left, weights, dims, preferred_element_type=F32)


def body(nrow, nth, rhs, dr, dt, mixm, mixo):
    V, K, RL, TL = rhs.shape
    sizes = (V, K, RL, TL, nrow, nth)
    nchunk = K // KC
    kr = KC * RL
    field = jax.ShapeDtypeStruct((V, K * RL, TL), F32)
    vmem = pl.BlockSpec(memory_space=pltpu.VMEM)
    hbm = pl.BlockSpec(memory_space=pl.ANY)
    mixm = mixm.reshape(V * V, K, RL)
    mixo = mixo.reshape(V * V, K, RL)
    dma = pltpu.SemaphoreType.DMA
    l2, infl, etab = pl.pallas_call(
        functools.partial(solve_kernel, sizes),
        out_shape=(
            field,
            jax.ShapeDtypeStruct((K, V, TL), F32),
            jax.ShapeDtypeStruct((K, 32, TL), F32),
        ),
        in_specs=[hbm, vmem, vmem, vmem, vmem],
        out_specs=(hbm, hbm, vmem),
        scratch_shapes=[
            pltpu.VMEM((nchunk, V, kr, TL), F32),
            pltpu.VMEM((V, kr, TL), F32),
            pltpu.VMEM((V, kr, TL), F32),
            pltpu.VMEM((nchunk, V, kr, TL), F32),
            pltpu.VMEM((V, kr, TL), F32),
            pltpu.VMEM((3, V, K, TL), F32),
            pltpu.VMEM((2, nchunk, RL, V * V, KC, TL), F32),
            pltpu.VMEM((K, V, TL, 2 * TL), BF16),
            pltpu.VMEM((K, 32, TL), F32),
            pltpu.VMEM((K, V * RL, TL), BF16),
            pltpu.VMEM((K, V * RL, TL), BF16),
            pltpu.VMEM((nchunk, nrow * SLOT, TL), F32),
            pltpu.VMEM((nchunk, nrow, SLOT, TL), F32),
            pltpu.VMEM((nchunk, nrow, SLOT, TL), F32),
            pltpu.VMEM((nchunk, nrow * SLOT, TL), F32),
            pltpu.VMEM((K, V, TL), F32),
            pltpu.VMEM((nth, V, TL), F32),
            pltpu.VMEM((nth, V, TL), F32),
            pltpu.VMEM((K, V, TL), F32),
            dma((nchunk,)), dma((nchunk,)), dma((nchunk,)), dma((nchunk,)), dma((nchunk,)),
            dma, dma, dma, dma, dma((nchunk,)), dma,
        ],
        compiler_params=pltpu.CompilerParams(
            collective_id=0, has_side_effects=True, vmem_limit_bytes=60 * 1024 * 1024
        ),
        name="solve",
    )(rhs.reshape(V, K * RL, TL), dr, dt, mixm, mixo)
    kb = KC
    out = pl.pallas_call(
        functools.partial(finish_kernel, sizes),
        grid=(K // kb,),
        out_shape=field,
        in_specs=[
            pl.BlockSpec((V, kb * RL, TL), lambda i: (0, i, 0)),
            pl.BlockSpec((kb, V, TL), lambda i: (i, 0, 0)),
            pl.BlockSpec((kb, 32, TL), lambda i: (i, 0, 0)),
            pl.BlockSpec((V * V, kb, RL), lambda i: (0, i, 0)),
        ],
        out_specs=pl.BlockSpec((V, kb * RL, TL), lambda i: (0, i, 0)),
        compiler_params=pltpu.CompilerParams(vmem_limit_bytes=32 * 1024 * 1024),
        name="finish",
    )(l2, infl, etab, mixo)
    return out.reshape(V, K, RL, TL)


def solution(mesh):
    return jax.shard_map(
        functools.partial(body, mesh.shape["row"], mesh.shape["theta"]),
        mesh=mesh,
        in_specs=(
            P(None, None, "row", "theta"),
            P(),
            P(),
            P(None, None, None, "row"),
            P(None, None, None, "row"),
        ),
        out_specs=P(None, None, "row", "theta"),
        check_vma=False,
    )
```

profile of v0, /device:TPU:1, one launch (start us, length us, event | category | flops | bytes accessed | tf_op | source)
XLA Modules:
  0.0 98.8 jit_solution(9836240439175243919)
XLA Ops:
  0.0 0.0 copy-start.1
  0.0 1.3 %copy.6.dr = f32[2,5,32]{2,1,0:T(8,128)} copy(f32[2,5,32]{2,0,1:T(2,128)} %param.6) | data formatting | bytes 2560 | tf_op args[1]
  1.3 1.3 %copy.7.dt = f32[2,5,32]{2,1,0:T(8,128)} copy(f32[2,5,32]{2,0,1:T(2,128)} %param.7) | data formatting | bytes 2560 | tf_op args[2]
  2.6 82.8 %solve.1 = (f32[5,1024,128]{2,1,0:T(8,128)}, f32[32,5,128]{2,1,0:T(8,128)}, f32[32,32,128]{2,1,0:T(8,128)}) custom-call(f32[5,1024,128]{2,1,0:T(8,128)} %bitcast.6, f32[2,5,32]{2,1,0:T(8,128)} %copy.6.dr, f32[2,5,32]{2,1,0:T(8,128)} %copy.7.dt, f32[25,32,32]{2,1,0:T(8,128)} %bitcast.7, f32[25,32,32]{2,1,0:T(8,128)} %bitcast.4), custom_call_target="tpu_custom_call" | custom-call | tf_op jit(solution)/shard_map/solve/pallas_call | solution.py:450
  85.4 0.0 copy-done.1
  85.4 0.0 copy-start
  85.4 1.7 %copy-done = f32[5,1024,128]{2,1,0:T(8,128)S(1)} copy-done((f32[5,1024,128]{2,1,0:T(8,128)S(1)}, f32[5,1024,128]{2,1,0:T(8,128)}, u32[]{:S(2)}) %copy-start) | copy-done | bytes 2621464
  87.1 0.0 copy-start.2
  87.1 1.0 %copy-done.2 = f32[32,32,128]{2,1,0:T(8,128)S(1)} copy-done((f32[32,32,128]{2,1,0:T(8,128)S(1)}, f32[32,32,128]{2,1,0:T(8,128)}, u32[]{:S(2)}) %copy-start.2) | copy-done | bytes 524312
  88.2 0.0 copy-start.3
  88.2 0.9 copy-done.3
  89.1 9.7 %finish.1 = f32[5,1024,128]{2,1,0:T(8,128)} custom-call(f32[5,1024,128]{2,1,0:T(8,128)S(1)} %copy-done, f32[32,5,128]{2,1,0:T(8,128)S(1)} %copy-done.3, f32[32,32,128]{2,1,0:T(8,128)S(1)} %copy-done.2, f32[25,32,32]{2,1,0:T(8,128)S(1)} %bitcast.5), custom_call_target="tpu_custom_call" | custom-call | tf_op jit(solution)/shard_map/finish/pallas_call | solution.py:488
Async XLA Ops:
  0.0 85.4 %copy-start.1 = (f32[5,5,32,32]{3,2,1,0:T(8,128)S(1)}, f32[5,5,32,32]{3,2,1,0:T(8,128)}, u32[]{:S(2)}) copy-start(f32[5,5,32,32]{3,2,1,0:T(8,128)} %param.9) | copy-start | bytes 307204
  85.4 1.7 %copy-start = (f32[5,1024,128]{2,1,0:T(8,128)S(1)}, f32[5,1024,128]{2,1,0:T(8,128)}, u32[]{:S(2)}) copy-start(f32[5,1024,128]{2,1,0:T(8,128)} %get-tuple-element.8.l2) | copy-start | bytes 7864324
  87.1 1.0 %copy-start.2 = (f32[32,32,128]{2,1,0:T(8,128)S(1)}, f32[32,32,128]{2,1,0:T(8,128)}, u32[]{:S(2)}) copy-start(f32[32,32,128]{2,1,0:T(8,128)} %get-tuple-element.10.etab) | copy-start | bytes 1572868
  88.2 0.9 copy-start.3
where the time goes:
time: 99.1 us; the launch traced here: 98.8 us
  Pallas kernels  92.5 us (93%)
  local copies, waits for them, and re-layouts  6.31 us (6%)
    pallas_call x1, Pallas kernels, body(): pl.pallas_call(functools.partial(solve_kernel, sizes), out_shape=(field,...  82.8 us
    pallas_call x1, Pallas kernels, body(): pl.pallas_call(functools.partial(finish_kernel, sizes), grid=(K // kb,),...  9.73 us
    unnamed x10, local copies, waits for them, and re-layouts  6.31 us

commit v1 on v0

v1 whole, which is shorter than its diff:
```python
import functools

import jax
import jax.numpy as jnp
from jax import lax
from jax.experimental import pallas as pl
from jax.experimental.pallas import tpu as pltpu
from jax.sharding import PartitionSpec as P

MESH = pl.DeviceIdType.MESH
KC = 8
SLOT = 24
STATES = 4
LINE = 32
F32 = jnp.float32
BF16 = jnp.bfloat16


def gap(u):
    h = 0.5 * u
    q = h * h
    series = 1.0 + q / 6.0 * (1.0 + q / 20.0 * (1.0 + q / 42.0 * (1.0 + q / 72.0)))
    return 2.0 * jnp.exp(-h) * h * series


def split(x):
    hi = x.astype(BF16)
    return hi, (x - hi.astype(F32)).astype(BF16)


def block_transfer(u1, u2, doublings):
    a, b = jnp.exp(-u1), jnp.exp(-u2)
    c = a
    q11, q12, q21, q22 = a, b, a, b
    for _ in range(doublings):
        x11, x12 = q11 * a + q12 * c, q12 * b
        x21, x22 = q21 * a + q22 * c, q22 * b
        q11, q12, q21, q22 = (
            q11 + a * x11,
            q12 + a * x12,
            q21 + c * x11 + b * x21,
            q22 + c * x12 + b * x22,
        )
        c = c * (a + b)
        a, b = a * a, b * b
    return a, b, c, q11, q12, q21, q22


def pick_lane(values, index):
    lane = lax.broadcasted_iota(jnp.int32, values.shape, 1)
    return jnp.sum(jnp.where(lane == index, values, 0.0), axis=1, keepdims=True)


def power_tables(u1, u2, n, bits):
    nf = n.astype(F32)
    a, b = jnp.exp(-nf * u1), jnp.exp(-nf * u2)
    ab, bb = jnp.exp(-u1), jnp.exp(-u2)
    pb = jnp.ones_like(ab)
    p = jnp.zeros_like(nf * u1)
    low = jnp.ones_like(p)
    for bit in range(bits):
        has = (n >> bit) & 1 == 1
        p = jnp.where(has, ab * p + low * pb, p)
        low = jnp.where(has, low * bb, low)
        pb = pb * (ab + bb)
        ab, bb = ab * ab, bb * bb
    return a, b, p


def solve_kernel(
    sizes, rhs, decay_r, decay_t, mixm, mixo, l2, infl, etab, gain,
    xin, xbuf, zbuf, ybuf, rcoef, ucol, h0tab, h1tab, wtab, wturn, gtab, mcat, mrows, xsplit,
    e1, rcv1, o1, rcv2, tx1, trc1, tx2, trc2,
    in_sem, s1s, s1r, s2s, s2r, t1s, t1r, t2s, t2r, fin_sem,
):
    V, K, RL, TL, nrow, nth = sizes
    nchunk = K // KC
    me_r = lax.axis_index("row")
    me_t = lax.axis_index("theta")
    kr = KC * RL
    dr = [decay_r[:, j, :] for j in range(2)]
    dt = [decay_t[:, j, :] for j in range(2)]

    def in_copy(c):
        return pltpu.make_async_copy(rhs.at[:, pl.ds(c * kr, kr), :], xin.at[c], in_sem.at[c])

    for c in range(nchunk):
        in_copy(c).start()

    barrier = pltpu.get_barrier_semaphore()

    @pl.loop(1, nrow)
    def _(d):
        pl.semaphore_signal(barrier, inc=1, device_id={"row": lax.rem(me_r + d, nrow)}, device_id_type=MESH)

    @pl.loop(1, nth)
    def _(d):
        pl.semaphore_signal(barrier, inc=1, device_id={"theta": lax.rem(me_t + d, nth)}, device_id_type=MESH)

    cells_r = RL * nrow
    ur1, ur2 = dr[0] / cells_r, dr[1] / cells_r
    fr = gap(ur1) * gap(ur2)
    diag = lax.broadcasted_iota(jnp.int32, (K, K), 0) == lax.broadcasted_iota(jnp.int32, (K, K), 1)

    def to_columns(table, ref, j):
        for m in range(V):
            column = jnp.sum(
                jnp.where(diag, jnp.broadcast_to(table[m : m + 1, :], (K, K)), 0.0), axis=1, keepdims=True
            )
            ref[j, m] = jnp.broadcast_to(column, (K, TL))

    for j, table in enumerate((jnp.exp(-ur1), jnp.exp(-ur2), fr * fr)):
        to_columns(table, rcoef, j)
    radial_block = block_transfer(ur1, ur2, RL.bit_length() - 1)

    def radial_pass(c, states, emit):
        r1 = [rcoef[0, m, pl.ds(c * KC, KC), :] for m in range(V)]
        r2 = [rcoef[1, m, pl.ds(c * KC, KC), :] for m in range(V)]

        def ahead(r, carry):
            out = []
            for m in range(V):
                s1, s2 = carry[m]
                s1 = r1[m] * s1 + xin[c, m, pl.ds(r, KC, stride=RL), :]
                s2 = r2[m] * s2 + s1
                ybuf[m, pl.ds(pl.multiple_of(r * KC, KC), KC), :] = s2
                out.append((s1, s2))
            return tuple(out)

        def behind(i, carry):
            r = RL - 1 - i
            out = []
            for m in range(V):
                u1, u2 = carry[m]
                u1 = r1[m] * u1 + ybuf[m, pl.ds(pl.multiple_of(r * KC, KC), KC), :]
                u2 = r2[m] * u2 + u1
                out.append((u1, u2))
            if emit is not None:
                emit(r, [pair[1] for pair in out])
            return tuple(out)

        first = lax.fori_loop(0, RL, ahead, tuple((s[0], s[1]) for s in states), unroll=8)
        second = lax.fori_loop(0, RL, behind, tuple((s[2], s[3]) for s in states), unroll=8)
        return first, second

    @pl.loop(0, nchunk)
    def _(c):
        in_copy(c).wait()
        zero = jnp.zeros((KC, TL), F32)
        first, second = radial_pass(c, [(zero,) * 4] * V, None)
        for m in range(V):
            for s, value in enumerate((first[m][0], first[m][1], second[m][0], second[m][1])):
                e1[c, pl.ds(s * V + m, KC, stride=SLOT), :] = value

    cells_t = TL * nth
    ut1, ut2 = dt[0] / cells_t, dt[1] / cells_t
    to_columns(ut1, ucol, 0)
    to_columns(ut2, ucol, 1)
    lane32 = lax.broadcasted_iota(jnp.int32, (RL, TL), 1)
    lane8 = lax.broadcasted_iota(jnp.int32, (8, TL), 1)
    bits = TL.bit_length() - 1
    etab[...] = jnp.zeros_like(etab)
    wtab[...] = jnp.zeros_like(wtab)

    def tables(q, carry):
        m, c = q // nchunk, q % nchunk
        rows = pl.ds(pl.multiple_of(c * KC, KC), KC)
        u1, u2 = ucol[0, m, rows, :], ucol[1, m, rows, :]
        r1, r2 = jnp.exp(-u1), jnp.exp(-u2)
        f = gap(u1) * gap(u2)
        i12, i11, i22 = 1.0 / gap(u1 + u2), 1.0 / gap(2.0 * u1), 1.0 / gap(2.0 * u2)
        scale_1 = f * f * r1 * i12
        coef_a = scale_1 * i12 * (r1 * i11 + r2 * i22)
        coef_p = scale_1 * i22
        coef_b = f * f * i12 * i22
        af, bf, pf = power_tables(u1, u2, lane8, bits)
        ar, br, pr = power_tables(u1, u2, TL - 1 - lane8, bits)
        pf1, pr1 = r1 * pf + bf, r1 * pr + br
        e_t1 = coef_a * (r1 * ar) + coef_p * pr1
        e_t2 = coef_b * (r2 * br)
        h0tab[m, rows, :] = coef_a * af + coef_p * pf + coef_b * bf
        h1tab[m, rows, :] = e_t1 + e_t2
        e_s1 = coef_a * (r1 * af) + coef_p * pf1
        e_s2 = coef_b * (r2 * bf)
        for s, value in enumerate((e_s1, e_s2, e_t1, e_t2)):
            etab[pl.ds(c * KC * 32 + 8 * s + m, KC, stride=32), :] = value
        for s, value in enumerate((ar, pr1, af, pf1)):
            wtab[pl.ds(c * KC * 32 + 8 * s + m, KC, stride=32), :] = value
        return carry

    lax.fori_loop(0, V * nchunk, tables, 0, unroll=2)

    tile = TL // LINE
    for j in range(K // tile):
        hi, lo = split(wtab[j * TL : (j + 1) * TL, :].T)
        wturn[j] = jnp.concatenate([hi, hi, lo], axis=0)

    for which, table in enumerate((mixm, mixo)):
        for m in range(V):
            four = jnp.concatenate([table[m * V + n] for n in range(V - 1)], axis=1)
            last = table[m * V + V - 1]
            four_hi = four.astype(BF16).astype(F32)
            last_hi = last.astype(BF16).astype(F32)
            last = jnp.concatenate([last_hi, last_hi, last - last_hi, jnp.zeros_like(last)], axis=1)
            mcat[which, m, :, 0:TL] = four_hi
            mcat[which, m, :, TL : 2 * TL] = four - four_hi
            mcat[which, m, :, 2 * TL : 3 * TL] = last
    on_diagonal = (
        lax.broadcasted_iota(jnp.int32, (RL, 3 * TL), 0) == lax.broadcasted_iota(jnp.int32, (RL, 3 * TL), 1) % RL
    )

    def mix(which, k, field):
        hi, lo = split(field)
        four = (V - 1) * RL
        right = jnp.concatenate(
            [hi[0:four], lo[0:four], hi[0:four], hi[four:], lo[four:], hi[four:], jnp.zeros((RL, TL), BF16)], axis=0
        )
        left = []
        for m in range(V):
            row = jnp.broadcast_to(mcat[which, m, pl.ds(k, 1), :], (RL, 3 * TL))
            left.append(jnp.where(on_diagonal, row, 0.0).astype(BF16))
        left = jnp.concatenate(left, axis=0)
        left = jnp.concatenate([left[:, 0:TL], left], axis=1)
        return jnp.dot(left, right, preferred_element_type=F32)

    pl.semaphore_wait(barrier, nrow - 1 + nth - 1)

    @pl.loop(0, nchunk)
    def _(c):
        @pl.loop(1, nrow)
        def _(d):
            p = lax.rem(me_r + d, nrow)
            pltpu.make_async_remote_copy(
                src_ref=e1.at[c, pl.ds(pl.multiple_of(p * SLOT, 8), SLOT), :],
                dst_ref=rcv1.at[c, me_r],
                send_sem=s1s.at[c],
                recv_sem=s1r.at[c],
                device_id={"row": p},
                device_id_type=MESH,
            ).start()

        pltpu.make_async_copy(
            e1.at[c, pl.ds(pl.multiple_of(me_r * SLOT, 8), SLOT), :], rcv1.at[c, me_r], s1r.at[c]
        ).start()

    lane16 = lax.broadcasted_iota(jnp.int32, (16, TL), 1)
    sub16 = lax.broadcasted_iota(jnp.int32, (16, TL), 0)

    def toeplitz(k):
        for m in range(V):
            near = pltpu.roll(jnp.broadcast_to(h0tab[m, pl.ds(k, 1), :], (16, TL)), 0, 1, stride=1, stride_axis=0)
            far = pltpu.roll(jnp.broadcast_to(h1tab[m, pl.ds(k, 1), :], (16, TL)), 0, 1, stride=1, stride_axis=0)
            near = jnp.where(lane16 < sub16, far, near)
            for part, (n, f) in enumerate(zip(split(near), split(far))):
                for b in range(TL // 16):
                    rows = pltpu.roll(jnp.where(lane16 >= TL - 16 * b, f, n), 16 * b, 1) if b else n
                    gtab[k, m, 16 * b : 16 * b + 16, part * TL : part * TL + TL] = rows

    ready = K * 9 // 16

    @pl.loop(0, ready)
    def _(k):
        toeplitz(k)

    mrows[...] = jnp.zeros_like(mrows)
    for m in range(V):
        for n in range(V):
            mrows[pl.ds(m * K * 8 + n, K, stride=8), 0:RL] = mixo[m * V + n]
    group = 8 * TL // LINE
    source = lax.broadcasted_iota(jnp.int32, (TL, TL), 0)
    target = lax.broadcasted_iota(jnp.int32, (TL, TL), 1)
    source_rows = 8 * (target // LINE) + target % 8
    turned = []
    for m in range(V):
        for j in range(K * 8 // TL):
            turned.append(mrows[pl.ds(m * K * 8 + j * TL, TL), :].T[0:RL])
    hi, lo = split(jnp.concatenate(turned, axis=0))
    halves = jnp.concatenate([hi, lo], axis=1)
    for q in range(TL // group):
        pick = jnp.where(source == source_rows + q * group, 1.0, 0.0).astype(BF16)
        spread_rows = jnp.dot(halves, jnp.concatenate([pick, pick], axis=0), preferred_element_type=F32)
        for m in range(V):
            for j in range(K * 8 // TL):
                i = m * (K * 8 // TL) + j
                gain[j * (TL // group) + q, m * RL : m * RL + RL, :] = spread_rows[i * RL : i * RL + RL]

    @pl.loop(0, nchunk)
    def _(c):
        a, b, cc, q11, q12, q21, q22 = (
            jnp.broadcast_to(pick_lane(x, c * KC + me_r), (V, TL)) for x in radial_block
        )
        pltpu.make_async_copy(rcv1.at[c], rcv1.at[c], s1r.at[c]).wait()

        def got(d, s):
            return rcv1[c, d, s * V : s * V + V, :]

        zero = jnp.zeros((V, TL), F32)
        sa, sb = [zero], [zero]
        for d in range(nrow - 1):
            sa.append(a * sa[d] + got(d, 0))
            sb.append(b * sb[d] + cc * sa[d] + got(d, 1))
        ta, tb = zero, zero
        for d in range(nrow - 1, -1, -1):
            for s, value in enumerate((sa[d], sb[d], ta, tb)):
                o1[c, d, s * V : s * V + V, :] = value
            if d:
                ta, tb = (
                    a * ta + got(d, 2) + q11 * sa[d] + q12 * sb[d],
                    b * tb + cc * ta + got(d, 3) + q21 * sa[d] + q22 * sb[d],
                )

        @pl.loop(1, nrow)
        def _(i):
            p = lax.rem(me_r + i, nrow)
            pltpu.make_async_remote_copy(
                src_ref=o1.at[c, p],
                dst_ref=rcv2.at[c, pl.ds(pl.multiple_of(me_r * SLOT, 8), SLOT), :],
                send_sem=s2s.at[c],
                recv_sem=s2r.at[c],
                device_id={"row": p},
                device_id_type=MESH,
            ).start()

        pltpu.make_async_copy(
            o1.at[c, me_r], rcv2.at[c, pl.ds(pl.multiple_of(me_r * SLOT, 8), SLOT), :], s2r.at[c]
        ).start()

    @pl.loop(ready, K)
    def _(k):
        toeplitz(k)

    @pl.loop(0, nchunk)
    def _(c):
        pltpu.make_async_copy(rcv2.at[c], rcv2.at[c], s2r.at[c]).wait()
        states = [
            tuple(rcv2[c, pl.ds(s * V + m, KC, stride=SLOT), :] for s in range(4)) for m in range(V)
        ]
        f2 = [rcoef[2, m, pl.ds(c * KC, KC), :] for m in range(V)]

        def emit(r, z):
            for m in range(V):
                xbuf[m, pl.ds(pl.multiple_of(r * KC, KC), KC), :] = f2[m] * z[m]

        radial_pass(c, states, emit)

        def leaving(j, carry):
            total = jnp.zeros((RL, TL), F32)
            for kk in range(tile):
                k = c * KC + j * tile + kk
                field = [xbuf[m, pl.ds(j * tile + kk, RL, stride=KC), :] for m in range(V)]
                hi, lo = split(mix(0, k, jnp.concatenate(field, axis=0)))
                xsplit[k, :, 0:TL] = hi
                xsplit[k, :, TL : 2 * TL] = lo
                out = jnp.dot(
                    jnp.concatenate([hi, lo, hi], axis=1), wturn[c * (KC // tile) + j], preferred_element_type=F32
                )
                for m in range(V):
                    mine = (lane32 // LINE == kk) & (lane32 % 8 == m)
                    total = total + jnp.where(mine, out[m * RL : m * RL + RL], 0.0)
            tx1[pl.ds(c * (KC // tile) + j, RL, stride=8), :] = total
            return carry

        lax.fori_loop(0, KC // tile, leaving, 0, unroll=True)

    @pl.loop(1, nth)
    def _(i):
        p = lax.rem(me_t + i, nth)
        pltpu.make_async_remote_copy(
            src_ref=tx1.at[pl.ds(pl.multiple_of(p * 8, 8), 8), :],
            dst_ref=trc1.at[me_t],
            send_sem=t1s,
            recv_sem=t1r,
            device_id={"theta": p},
            device_id_type=MESH,
        ).start()

    pltpu.make_async_copy(tx1.at[pl.ds(pl.multiple_of(me_t * 8, 8), 8), :], trc1.at[me_t], t1r).start()

    def local_solve(c):
        def solve(kk, carry):
            k = c * KC + kk
            for m in range(V):
                hi = xsplit[k, m * RL : m * RL + RL, 0:TL]
                lo = xsplit[k, m * RL : m * RL + RL, TL : 2 * TL]
                z = jnp.dot(jnp.concatenate([hi, lo], axis=0), gtab[k, m], preferred_element_type=F32)
                z = z[0:RL, 0:TL] + z[RL : 2 * RL, 0:TL] + z[0:RL, TL : 2 * TL]
                zbuf[m, pl.ds(pl.multiple_of(kk * RL, RL), RL), :] = z
            return carry

        lax.fori_loop(0, KC, solve, 0, unroll=4)

        def out_mix(kk, carry):
            rows = pl.ds(pl.multiple_of(kk * RL, RL), RL)
            field = mix(1, c * KC + kk, jnp.concatenate([zbuf[n, rows, :] for n in range(V)], axis=0))
            for m in range(V):
                l2[m, pl.ds(pl.multiple_of((c * KC + kk) * RL, RL), RL), :] = field[m * RL : m * RL + RL]
            return carry

        lax.fori_loop(0, KC, out_mix, 0, unroll=4)

    local_solve(0)

    u1, u2 = jnp.ones((8, TL), F32), jnp.ones((8, TL), F32)
    for kk in range(tile):
        for m in range(V):
            mine = (lane8 // LINE == kk) & (lane8 % 8 == m)
            u1 = jnp.where(mine, ucol[0, m, pl.ds(kk, 8, stride=tile), :], u1)
            u2 = jnp.where(mine, ucol[1, m, pl.ds(kk, 8, stride=tile), :], u2)
    a, b, cc = block_transfer(u1, u2, bits)[:3]
    around_1 = 1.0 / (1.0 - jnp.exp(-cells_t * u1))
    around_2 = 1.0 / (1.0 - jnp.exp(-cells_t * u2))
    pltpu.make_async_copy(trc1, trc1, t1r).wait()
    forward = lane8 % LINE < LINE // 2
    entering = [jnp.where(forward, trc1[i], trc1[nth - 1 - i]) for i in range(nth)]

    def cycle(rate, decay, around, terms):
        chain = [jnp.zeros((8, TL), F32)]
        for i in range(nth):
            chain.append(rate * chain[i] + terms[i])
        start = chain[nth] * around
        return [chain[i] + jnp.exp(-(TL * i) * decay) * start for i in range(nth)]

    one = cycle(a, u1, around_1, entering)
    two = cycle(b, u2, around_2, [entering[i] + cc * pltpu.roll(one[i], 8, 1) for i in range(nth)])
    even = lane8 // 8 % 2 == 0
    state = [jnp.where(even, one[i], two[i]) for i in range(nth)]
    for d in range(nth):
        tx2[d] = jnp.where(forward, state[d], state[nth - 1 - d])

    @pl.loop(1, nth)
    def _(i):
        d = lax.rem(me_t + i, nth)
        pltpu.make_async_remote_copy(
            src_ref=tx2.at[d],
            dst_ref=trc2.at[pl.ds(pl.multiple_of(me_t * 8, 8), 8), :],
            send_sem=t2s,
            recv_sem=t2r,
            device_id={"theta": d},
            device_id_type=MESH,
        ).start()

    pltpu.make_async_copy(tx2.at[me_t], trc2.at[pl.ds(pl.multiple_of(me_t * 8, 8), 8), :], t2r).start()

    @pl.loop(1, nchunk)
    def _(c):
        local_solve(c)

    pltpu.make_async_copy(trc2, trc2, t2r).wait()
    final = pltpu.make_async_copy(trc2, infl, fin_sem)
    final.start()

    @pl.loop(0, nchunk)
    def _(c):
        sent = rcv1.at[c, pl.ds(0, nrow - 1)]
        pltpu.make_async_copy(sent, sent, s1s.at[c]).wait()
        pltpu.make_async_copy(sent, sent, s2s.at[c]).wait()

    sent = trc1.at[pl.ds(0, nth - 1)]
    pltpu.make_async_copy(sent, sent, t1s).wait()
    pltpu.make_async_copy(sent, sent, t2s).wait()
    final.wait()


def finish_kernel(sizes, l2, infl, etab, gain, out, buf, sem):
    V, K, RL, TL, nrow, nth = sizes
    tile = TL // LINE
    kr = tile * RL
    row = lax.broadcasted_iota(jnp.int32, (TL, TL), 0) // LINE

    def out_copy(j):
        rows = pl.ds(pl.multiple_of(j * kr, kr), kr)
        return pltpu.make_async_copy(buf.at[:, rows, :], out.at[:, rows, :], sem.at[j])

    @pl.loop(0, K // tile)
    def _(j):
        state = infl[pl.ds(j, RL, stride=8), :]
        hi, lo = split(gain[j] * jnp.concatenate([state] * V, axis=0))
        left = jnp.concatenate([hi, lo, hi], axis=1)
        response = etab[pl.ds(pl.multiple_of(j * TL, TL), TL), :]
        for kk in range(tile):
            ehi, elo = split(jnp.where(row == kk, response, 0.0))
            inflow = jnp.dot(left, jnp.concatenate([ehi, ehi, elo], axis=0), preferred_element_type=F32)
            rows = pl.ds(pl.multiple_of(j * kr + kk * RL, RL), RL)
            for m in range(V):
                buf[m, rows, :] = l2[m, rows, :] + inflow[m * RL : m * RL + RL]
        out_copy(j).start()

    @pl.loop(0, K // tile)
    def _(j):
        out_copy(j).wait()


def body(nrow, nth, rhs, dr, dt, mixm, mixo):
    V, K, RL, TL = rhs.shape
    sizes = (V, K, RL, TL, nrow, nth)
    nchunk = K // KC
    kr = KC * RL
    field = jax.ShapeDtypeStruct((V, K * RL, TL), F32)
    vmem = pl.BlockSpec(memory_space=pltpu.VMEM)
    hbm = pl.BlockSpec(memory_space=pl.ANY)
    mixm = mixm.reshape(V * V, K, RL)
    mixo = mixo.reshape(V * V, K, RL)
    dma = pltpu.SemaphoreType.DMA
    nline = K * LINE // TL
    l2, infl, etab, gain = pl.pallas_call(
        functools.partial(solve_kernel, sizes),
        out_shape=(
            pltpu.VMEM((V, K * RL, TL), F32),
            pltpu.VMEM((nth * 8, TL), F32),
            pltpu.VMEM((K * LINE, TL), F32),
            pltpu.VMEM((nline, V * RL, TL), F32),
        ),
        in_specs=[pl.BlockSpec(memory_space=pltpu.HBM), vmem, vmem, vmem, vmem],
        out_specs=(vmem, vmem, vmem, vmem),
        scratch_shapes=[
            pltpu.VMEM((nchunk, V, kr, TL), F32),
            pltpu.VMEM((V, kr, TL), F32),
            pltpu.VMEM((V, kr, TL), F32),
            pltpu.VMEM((V, kr, TL), F32),
            pltpu.VMEM((3, V, K, TL), F32),
            pltpu.VMEM((2, V, K, TL), F32),
            pltpu.VMEM((V, K, TL), F32),
            pltpu.VMEM((V, K, TL), F32),
            pltpu.VMEM((K * LINE, TL), F32),
            pltpu.VMEM((nline, 3 * TL, TL), BF16),
            pltpu.VMEM((K, V, TL, 2 * TL), BF16),
            pltpu.VMEM((2, V, K, 3 * TL), F32),
            pltpu.VMEM((V * K * 8, TL), F32),
            pltpu.VMEM((K, V * RL, 2 * TL), BF16),
            pltpu.VMEM((nchunk, nrow * SLOT, TL), F32),
            pltpu.VMEM((nchunk, nrow, SLOT, TL), F32),
            pltpu.VMEM((nchunk, nrow, SLOT, TL), F32),
            pltpu.VMEM((nchunk, nrow * SLOT, TL), F32),
            pltpu.VMEM((RL * 8, TL), F32),
            pltpu.VMEM((nth, 8, TL), F32),
            pltpu.VMEM((nth, 8, TL), F32),
            pltpu.VMEM((nth * 8, TL), F32),
            dma((nchunk,)), dma((nchunk,)), dma((nchunk,)), dma((nchunk,)), dma((nchunk,)),
            dma, dma, dma, dma, dma,
        ],
        compiler_params=pltpu.CompilerParams(
            collective_id=0, has_side_effects=True, vmem_limit_bytes=58 * 1024 * 1024
        ),
        name="solve",
    )(rhs.reshape(V, K * RL, TL), jnp.swapaxes(dr, 0, 1), jnp.swapaxes(dt, 0, 1), mixm, mixo)
    out = pl.pallas_call(
        functools.partial(finish_kernel, sizes),
        out_shape=field,
        in_specs=[vmem, vmem, vmem, vmem],
        out_specs=hbm,
        scratch_shapes=[pltpu.VMEM((V, K * RL, TL), F32), dma((K * LINE // TL,))],
        compiler_params=pltpu.CompilerParams(vmem_limit_bytes=16 * 1024 * 1024),
        name="finish",
    )(l2, infl, etab, gain)
    return out.reshape(V, K, RL, TL)


def solution(mesh):
    return jax.shard_map(
        functools.partial(body, mesh.shape["row"], mesh.shape["theta"]),
        mesh=mesh,
        in_specs=(
            P(None, None, "row", "theta"),
            P(),
            P(),
            P(None, None, None, "row"),
            P(None, None, None, "row"),
        ),
        out_specs=P(None, None, "row", "theta"),
        check_vma=False,
    )
```

time: 99.1 us -> 49.1 us (0.50)
  Pallas kernels: 92.5 us -> 49 us
  local copies, waits for them, and re-layouts: 6.31 us -> 0 us
    pallas_call x2, Pallas kernels: 92.5 us -> 49 us  [the longest x1 46 us: body(): pl.pallas_call(functools.partial(solve_kernel, sizes), out_shape=(pltpu.V...]
    unnamed x10 -> x0, local copies, waits for them, and re-layouts: 6.31 us -> none
where the time goes in v1:
time: 49.1 us; the launch traced here: 49 us
  Pallas kernels  49 us (100%)
    pallas_call x1, Pallas kernels, body(): pl.pallas_call(functools.partial(solve_kernel, sizes), out_shape=(pltpu.V...  46 us
    pallas_call x1, Pallas kernels, body(): pl.pallas_call(functools.partial(finish_kernel, sizes), out_shape=field,...  3.07 us

profile of v1, /device:TPU:1, one launch (start us, length us, event | category | flops | bytes accessed | tf_op | source)
XLA Modules:
  0.0 49.0 jit_solution(4770969487676373283)
XLA Ops:
  0.0 46.0 %solve.1 = (f32[5,1024,128]{2,1,0:T(8,128)S(1)}, f32[256,128]{1,0:T(8,128)S(1)}, f32[1024,128]{1,0:T(8,128)S(1)}, f32[8,160,128]{2,1,0:T(8,128)S(1)}) custom-call(f32[5,1024,128]{2,1,0:T(8,128)} %bitcast.6, f32[5,2,32]{2,1,0:T(2,128)} %bitcast.9, f32[5,2,32]{2,1,0:T(2,128)} %bitcast.10, f32[25,32,32]{2,1,0:T(8,128)} %bitcast.7, f32[25,32,32]{2,1,0:T(8,128)} %bitcast.8), custom_call_target="tpu_custom_call" | custom-call | tf_op jit(solution)/shard_map/solve/pallas_call | solution.py:505
  46.0 3.1 %finish.1 = f32[5,1024,128]{2,1,0:T(8,128)} custom-call(f32[5,1024,128]{2,1,0:T(8,128)S(1)} %get-tuple-element.9.l2, f32[256,128]{1,0:T(8,128)S(1)} %get-tuple-element.10.infl, f32[1024,128]{1,0:T(8,128)S(1)} %get-tuple-element.11.etab, f32[8,160,128]{2,1,0:T(8,128)S(1)} %get-tuple-element.12.gain), custom_call_target="tpu_custom_call" | custom-call | tf_op jit(solution)/shard_map/finish/pallas_call | solution.py:546

commit v2 on v1

--- a/solution.py
+++ b/solution.py
@@ -9,11 +9,24 @@
 
 MESH = pl.DeviceIdType.MESH
 KC = 8
-SLOT = 24
+SLOT, USED = 24, 20
 STATES = 4
+CUT_1, CUT_2 = 0, 16
 LINE = 32
 F32 = jnp.float32
 BF16 = jnp.bfloat16
+
+
+def row_peer(me, i, n):
+    half = n // 2
+    step = jnp.where(i < half, i, i - half)
+    shift = lax.rem(half // 2 + jnp.where(step % 2 == 0, half - step // 2, (step + 1) // 2), half)
+    side = jnp.where(i < half, me // half + 1, me // half) % 2
+    return side * half + lax.rem(me + shift, half)
+
+
+def theta_peer(me, i, n):
+    return lax.rem(me + n // 2 + jnp.where(i % 2 == 0, n - i // 2, (i + 1) // 2), n)
 
 
 def gap(u):
@@ -69,9 +82,9 @@
 
 def solve_kernel(
     sizes, rhs, decay_r, decay_t, mixm, mixo, l2, infl, etab, gain,
-    xin, xbuf, zbuf, ybuf, rcoef, ucol, h0tab, h1tab, wtab, wturn, gtab, mcat, mrows, xsplit,
-    e1, rcv1, o1, rcv2, tx1, trc1, tx2, trc2,
-    in_sem, s1s, s1r, s2s, s2r, t1s, t1r, t2s, t2r, fin_sem,
+    xin, xbuf, zbuf, ybuf, rcoef, ucol, h0tab, h1tab, wtab, wturn, gtab, mcoef, mflat, mcat, mrows, xsplit, xt,
+    e1, rcv1, o1, rcv2, tx1, trc1, tx2,
+    in_sem, s1s, s1r, s2s, s2r, t1s, t1r, t2s, t2r,
 ):
     V, K, RL, TL, nrow, nth = sizes
     nchunk = K // KC
@@ -89,13 +102,13 @@
 
     barrier = pltpu.get_barrier_semaphore()
 
-    @pl.loop(1, nrow)
-    def _(d):
-        pl.semaphore_signal(barrier, inc=1, device_id={"row": lax.rem(me_r + d, nrow)}, device_id_type=MESH)
-
-    @pl.loop(1, nth)
-    def _(d):
-        pl.semaphore_signal(barrier, inc=1, device_id={"theta": lax.rem(me_t + d, nth)}, device_id_type=MESH)
+    @pl.loop(0, nth - 1)
+    def _(i):
+        pl.semaphore_signal(barrier, inc=1, device_id={"theta": theta_peer(me_t, i, nth)}, device_id_type=MESH)
+
+    @pl.loop(0, nrow - 1)
+    def _(i):
+        pl.semaphore_signal(barrier, inc=1, device_id={"row": row_peer(me_r, i, nrow)}, device_id_type=MESH)
 
     cells_r = RL * nrow
     ur1, ur2 = dr[0] / cells_r, dr[1] / cells_r
@@ -121,7 +134,7 @@
             out = []
             for m in range(V):
                 s1, s2 = carry[m]
-                s1 = r1[m] * s1 + xin[c, m, pl.ds(r, KC, stride=RL), :]
+                s1 = r1[m] * s1 + xt[c, m, pl.ds(pl.multiple_of(r * KC, KC), KC), :]
                 s2 = r2[m] * s2 + s1
                 ybuf[m, pl.ds(pl.multiple_of(r * KC, KC), KC), :] = s2
                 out.append((s1, s2))
@@ -146,11 +159,39 @@
     @pl.loop(0, nchunk)
     def _(c):
         in_copy(c).wait()
+
+        @pl.loop(0, V)
+        def _(m):
+            for kk in range(KC):
+                for q in range(RL // 8):
+                    first_row = kk * RL + q * 8
+                    xt[c, m, pl.ds(q * 8 * KC + kk, 8, stride=KC), :] = xin[c, m, first_row : first_row + 8, :]
+
         zero = jnp.zeros((KC, TL), F32)
         first, second = radial_pass(c, [(zero,) * 4] * V, None)
         for m in range(V):
             for s, value in enumerate((first[m][0], first[m][1], second[m][0], second[m][1])):
                 e1[c, pl.ds(s * V + m, KC, stride=SLOT), :] = value
+
+    pl.semaphore_wait(barrier, nrow - 1 + nth - 1)
+
+    @pl.loop(0, nchunk)
+    def _(c):
+        @pl.loop(0, nrow - 1)
+        def _(i):
+            p = row_peer(me_r, i, nrow)
+            pltpu.make_async_remote_copy(
+                src_ref=e1.at[c, pl.ds(pl.multiple_of(p * SLOT, 8), USED), :],
+                dst_ref=rcv1.at[c, me_r, pl.ds(0, USED), :],
+                send_sem=s1s.at[c],
+                recv_sem=s1r.at[c],
+                device_id={"row": p},
+                device_id_type=MESH,
+            ).start()
+
+        pltpu.make_async_copy(
+            e1.at[c, pl.ds(pl.multiple_of(me_r * SLOT, 8), USED), :], rcv1.at[c, me_r, pl.ds(0, USED), :], s1r.at[c]
+        ).start()
 
     cells_t = TL * nth
     ut1, ut2 = dt[0] / cells_t, dt[1] / cells_t
@@ -193,55 +234,48 @@
     tile = TL // LINE
     for j in range(K // tile):
         hi, lo = split(wtab[j * TL : (j + 1) * TL, :].T)
-        wturn[j] = jnp.concatenate([hi, hi, lo], axis=0)
-
-    for which, table in enumerate((mixm, mixo)):
+        wturn[j] = jnp.concatenate(
+            [jnp.concatenate([hi, hi], axis=0), jnp.concatenate([lo, jnp.zeros_like(lo)], axis=0)], axis=1
+        )
+
+    hi, lo = split(mixm.reshape(V * V * K, RL)[...])
+    halves = jnp.concatenate([hi, lo], axis=1)
+    pick_row = lax.broadcasted_iota(jnp.int32, (2 * RL, 2 * TL), 0) % RL
+    pick_half = lax.broadcasted_iota(jnp.int32, (2 * RL, 2 * TL), 1) // TL
+
+    @pl.loop(0, RL // 2)
+    def _(i):
+        pick = jnp.where(pick_row == 2 * i + pick_half, 1.0, 0.0).astype(BF16)
+        both = jnp.dot(halves, pick, preferred_element_type=F32)
+        mcoef[2 * i] = both[:, 0:TL]
+        mcoef[2 * i + 1] = both[:, TL : 2 * TL]
+
+    for m in range(V):
+        four = jnp.concatenate([mixo[m * V + n] for n in range(V - 1)], axis=1)
+        last = mixo[m * V + V - 1]
+        four_hi = four.astype(BF16).astype(F32)
+        last_hi = last.astype(BF16).astype(F32)
+        last = jnp.concatenate([last_hi, last_hi, last - last_hi, jnp.zeros_like(last)], axis=1)
+        mflat[m] = jnp.concatenate([four_hi, four - four_hi, last], axis=1)
+
+    @pl.loop(0, K)
+    def _(k):
         for m in range(V):
-            four = jnp.concatenate([table[m * V + n] for n in range(V - 1)], axis=1)
-            last = table[m * V + V - 1]
-            four_hi = four.astype(BF16).astype(F32)
-            last_hi = last.astype(BF16).astype(F32)
-            last = jnp.concatenate([last_hi, last_hi, last - last_hi, jnp.zeros_like(last)], axis=1)
-            mcat[which, m, :, 0:TL] = four_hi
-            mcat[which, m, :, TL : 2 * TL] = four - four_hi
-            mcat[which, m, :, 2 * TL : 3 * TL] = last
-    on_diagonal = (
-        lax.broadcasted_iota(jnp.int32, (RL, 3 * TL), 0) == lax.broadcasted_iota(jnp.int32, (RL, 3 * TL), 1) % RL
-    )
-
-    def mix(which, k, field):
+            mcat[k, m] = jnp.broadcast_to(mflat[m, pl.ds(k, 1), :], (16, 3 * TL)).astype(BF16)
+
+    row16 = lax.broadcasted_iota(jnp.int32, (16, 3 * TL), 0)
+    col16 = lax.broadcasted_iota(jnp.int32, (16, 3 * TL), 1) % RL
+    on_diagonal = [jnp.where(row16 + 16 * half == col16, 1.0, 0.0).astype(BF16) for half in range(RL // 16)]
+
+    def mix(k, field):
         hi, lo = split(field)
         four = (V - 1) * RL
         right = jnp.concatenate(
             [hi[0:four], lo[0:four], hi[0:four], hi[four:], lo[four:], hi[four:], jnp.zeros((RL, TL), BF16)], axis=0
         )
-        left = []
-        for m in range(V):
-            row = jnp.broadcast_to(mcat[which, m, pl.ds(k, 1), :], (RL, 3 * TL))
-            left.append(jnp.where(on_diagonal, row, 0.0).astype(BF16))
-        left = jnp.concatenate(left, axis=0)
+        left = jnp.concatenate([mcat[k, m] * mask for m in range(V) for mask in on_diagonal], axis=0)
         left = jnp.concatenate([left[:, 0:TL], left], axis=1)
         return jnp.dot(left, right, preferred_element_type=F32)
-
-    pl.semaphore_wait(barrier, nrow - 1 + nth - 1)
-
-    @pl.loop(0, nchunk)
-    def _(c):
-        @pl.loop(1, nrow)
-        def _(d):
-            p = lax.rem(me_r + d, nrow)
-            pltpu.make_async_remote_copy(
-                src_ref=e1.at[c, pl.ds(pl.multiple_of(p * SLOT, 8), SLOT), :],
-                dst_ref=rcv1.at[c, me_r],
-                send_sem=s1s.at[c],
-                recv_sem=s1r.at[c],
-                device_id={"row": p},
-                device_id_type=MESH,
-            ).start()
-
-        pltpu.make_async_copy(
-            e1.at[c, pl.ds(pl.multiple_of(me_r * SLOT, 8), SLOT), :], rcv1.at[c, me_r], s1r.at[c]
-        ).start()
 
     lane16 = lax.broadcasted_iota(jnp.int32, (16, TL), 1)
     sub16 = lax.broadcasted_iota(jnp.int32, (16, TL), 0)
@@ -256,11 +290,132 @@
                     rows = pltpu.roll(jnp.where(lane16 >= TL - 16 * b, f, n), 16 * b, 1) if b else n
                     gtab[k, m, 16 * b : 16 * b + 16, part * TL : part * TL + TL] = rows
 
-    ready = K * 9 // 16
-
-    @pl.loop(0, ready)
-    def _(k):
-        toeplitz(k)
+    def some_toeplitz(first, last):
+        @pl.loop(first, last)
+        def _(k):
+            toeplitz(k)
+
+    some_toeplitz(0, CUT_1)
+
+    @pl.loop(0, nchunk)
+    def _(c):
+        a, b, cc, q11, q12, q21, q22 = (
+            jnp.broadcast_to(pick_lane(x, c * KC + me_r), (V, TL)) for x in radial_block
+        )
+        arrived = rcv1.at[c, :, pl.ds(0, USED), :]
+        pltpu.make_async_copy(arrived, arrived, s1r.at[c]).wait()
+
+        def got(d, s):
+            return rcv1[c, d, s * V : s * V + V, :]
+
+        zero = jnp.zeros((V, TL), F32)
+        sa, sb = [zero], [zero]
+        for d in range(nrow - 1):
+            sa.append(a * sa[d] + got(d, 0))
+            sb.append(b * sb[d] + cc * sa[d] + got(d, 1))
+        ta, tb = zero, zero
+        for d in range(nrow - 1, -1, -1):
+            for s, value in enumerate((sa[d], sb[d], ta, tb)):
+                o1[c, d, s * V : s * V + V, :] = value
+            if d:
+                ta, tb = (
+                    a * ta + got(d, 2) + q11 * sa[d] + q12 * sb[d],
+                    b * tb + cc * ta + got(d, 3) + q21 * sa[d] + q22 * sb[d],
+                )
+
+        @pl.loop(0, nrow - 1)
+        def _(i):
+            p = row_peer(me_r, i, nrow)
+            pltpu.make_async_remote_copy(
+                src_ref=o1.at[c, p, pl.ds(0, USED), :],
+                dst_ref=rcv2.at[c, pl.ds(pl.multiple_of(me_r * SLOT, 8), USED), :],
+                send_sem=s2s.at[c],
+                recv_sem=s2r.at[c],
+                device_id={"row": p},
+                device_id_type=MESH,
+            ).start()
+
+        pltpu.make_async_copy(
+            o1.at[c, me_r, pl.ds(0, USED), :], rcv2.at[c, pl.ds(pl.multiple_of(me_r * SLOT, 8), USED), :], s2r.at[c]
+        ).start()
+
+    some_toeplitz(CUT_1, CUT_2)
+
+    @pl.loop(0, nchunk)
+    def _(c):
+        arrived = rcv2.at[c, pl.ds(0, nrow * USED), :]
+        pltpu.make_async_copy(arrived, arrived, s2r.at[c]).wait()
+        states = [
+            tuple(rcv2[c, pl.ds(s * V + m, KC, stride=SLOT), :] for s in range(4)) for m in range(V)
+        ]
+        f2 = [rcoef[2, m, pl.ds(c * KC, KC), :] for m in range(V)]
+
+        def emit(r, z):
+            z = [f2[m] * z[m] for m in range(V)]
+            for m in range(V):
+                total = None
+                for n in range(V):
+                    term = mcoef[r, pl.ds(pl.multiple_of((m * V + n) * K + c * KC, KC), KC), :] * z[n]
+                    total = term if total is None else total + term
+                xbuf[m, pl.ds(pl.multiple_of(r * KC, KC), KC), :] = total
+
+        radial_pass(c, states, emit)
+
+        def leaving(j, carry):
+            total = jnp.zeros((RL, TL), F32)
+            for kk in range(tile):
+                k = c * KC + j * tile + kk
+                field = [xbuf[m, pl.ds(j * tile + kk, RL, stride=KC), :] for m in range(V)]
+                hi, lo = split(jnp.concatenate(field, axis=0))
+                xsplit[k, :, 0:TL] = hi
+                xsplit[k, :, TL : 2 * TL] = lo
+                out = jnp.dot(
+                    jnp.concatenate([hi, lo], axis=1), wturn[c * (KC // tile) + j], preferred_element_type=F32
+                )
+                out = out[:, 0:TL] + out[:, TL : 2 * TL]
+                for m in range(V):
+                    mine = (lane32 // LINE == kk) & (lane32 % 8 == m)
+                    total = total + jnp.where(mine, out[m * RL : m * RL + RL], 0.0)
+            tx1[pl.ds(c * (KC // tile) + j, RL, stride=8), :] = total
+            return carry
+
+        lax.fori_loop(0, KC // tile, leaving, 0, unroll=True)
+
+    @pl.loop(0, nth - 1)
+    def _(i):
+        p = theta_peer(me_t, i, nth)
+        pltpu.make_async_remote_copy(
+            src_ref=tx1.at[pl.ds(pl.multiple_of(p * 8, 8), 8), :],
+            dst_ref=trc1.at[me_t],
+            send_sem=t1s,
+            recv_sem=t1r,
+            device_id={"theta": p},
+            device_id_type=MESH,
+        ).start()
+
+    pltpu.make_async_copy(tx1.at[pl.ds(pl.multiple_of(me_t * 8, 8), 8), :], trc1.at[me_t], t1r).start()
+
+    def local_solve(c):
+        def solve(kk, carry):
+            k = c * KC + kk
+            for m in range(V):
+                hi = xsplit[k, m * RL : m * RL + RL, 0:TL]
+                lo = xsplit[k, m * RL : m * RL + RL, TL : 2 * TL]
+                z = jnp.dot(jnp.concatenate([hi, lo], axis=0), gtab[k, m], preferred_element_type=F32)
+                z = z[0:RL, 0:TL] + z[RL : 2 * RL, 0:TL] + z[0:RL, TL : 2 * TL]
+                zbuf[m, pl.ds(pl.multiple_of(kk * RL, RL), RL), :] = z
+            return carry
+
+        lax.fori_loop(0, KC, solve, 0, unroll=4)
+
+        def out_mix(kk, carry):
+            rows = pl.ds(pl.multiple_of(kk * RL, RL), RL)
+            field = mix(c * KC + kk, jnp.concatenate([zbuf[n, rows, :] for n in range(V)], axis=0))
+            for m in range(V):
+                l2[m, pl.ds(pl.multiple_of((c * KC + kk) * RL, RL), RL), :] = field[m * RL : m * RL + RL]
+            return carry
+
+        lax.fori_loop(0, KC, out_mix, 0, unroll=4)
 
     mrows[...] = jnp.zeros_like(mrows)
     for m in range(V):
@@ -284,120 +439,7 @@
                 i = m * (K * 8 // TL) + j
                 gain[j * (TL // group) + q, m * RL : m * RL + RL, :] = spread_rows[i * RL : i * RL + RL]
 
-    @pl.loop(0, nchunk)
-    def _(c):
-        a, b, cc, q11, q12, q21, q22 = (
-            jnp.broadcast_to(pick_lane(x, c * KC + me_r), (V, TL)) for x in radial_block
-        )
-        pltpu.make_async_copy(rcv1.at[c], rcv1.at[c], s1r.at[c]).wait()
-
-        def got(d, s):
-            return rcv1[c, d, s * V : s * V + V, :]
-
-        zero = jnp.zeros((V, TL), F32)
-        sa, sb = [zero], [zero]
-        for d in range(nrow - 1):
-            sa.append(a * sa[d] + got(d, 0))
-            sb.append(b * sb[d] + cc * sa[d] + got(d, 1))
-        ta, tb = zero, zero
-        for d in range(nrow - 1, -1, -1):
-            for s, value in enumerate((sa[d], sb[d], ta, tb)):
-                o1[c, d, s * V : s * V + V, :] = value
-            if d:
-                ta, tb = (
-                    a * ta + got(d, 2) + q11 * sa[d] + q12 * sb[d],
-                    b * tb + cc * ta + got(d, 3) + q21 * sa[d] + q22 * sb[d],
-                )
-
-        @pl.loop(1, nrow)
-        def _(i):
-            p = lax.rem(me_r + i, nrow)
-            pltpu.make_async_remote_copy(
-                src_ref=o1.at[c, p],
-                dst_ref=rcv2.at[c, pl.ds(pl.multiple_of(me_r * SLOT, 8), SLOT), :],
-                send_sem=s2s.at[c],
-                recv_sem=s2r.at[c],
-                device_id={"row": p},
-                device_id_type=MESH,
-            ).start()
-
-        pltpu.make_async_copy(
-            o1.at[c, me_r], rcv2.at[c, pl.ds(pl.multiple_of(me_r * SLOT, 8), SLOT), :], s2r.at[c]
-        ).start()
-
-    @pl.loop(ready, K)
-    def _(k):
-        toeplitz(k)
-
-    @pl.loop(0, nchunk)
-    def _(c):
-        pltpu.make_async_copy(rcv2.at[c], rcv2.at[c], s2r.at[c]).wait()
-        states = [
-            tuple(rcv2[c, pl.ds(s * V + m, KC, stride=SLOT), :] for s in range(4)) for m in range(V)
-        ]
-        f2 = [rcoef[2, m, pl.ds(c * KC, KC), :] for m in range(V)]
-
-        def emit(r, z):
-            for m in range(V):
-                xbuf[m, pl.ds(pl.multiple_of(r * KC, KC), KC), :] = f2[m] * z[m]
-
-        radial_pass(c, states, emit)
-
-        def leaving(j, carry):
-            total = jnp.zeros((RL, TL), F32)
-            for kk in range(tile):
-                k = c * KC + j * tile + kk
-                field = [xbuf[m, pl.ds(j * tile + kk, RL, stride=KC), :] for m in range(V)]
-                hi, lo = split(mix(0, k, jnp.concatenate(field, axis=0)))
-                xsplit[k, :, 0:TL] = hi
-                xsplit[k, :, TL : 2 * TL] = lo
-                out = jnp.dot(
-                    jnp.concatenate([hi, lo, hi], axis=1), wturn[c * (KC // tile) + j], preferred_element_type=F32
-                )
-                for m in range(V):
-                    mine = (lane32 // LINE == kk) & (lane32 % 8 == m)
-                    total = total + jnp.where(mine, out[m * RL : m * RL + RL], 0.0)
-            tx1[pl.ds(c * (KC // tile) + j, RL, stride=8), :] = total
-            return carry
-
-        lax.fori_loop(0, KC // tile, leaving, 0, unroll=True)
-
-    @pl.loop(1, nth)
-    def _(i):
-        p = lax.rem(me_t + i, nth)
-        pltpu.make_async_remote_copy(
-            src_ref=tx1.at[pl.ds(pl.multiple_of(p * 8, 8), 8), :],
-            dst_ref=trc1.at[me_t],
-            send_sem=t1s,
-            recv_sem=t1r,
-            device_id={"theta": p},
-            device_id_type=MESH,
-        ).start()
-
-    pltpu.make_async_copy(tx1.at[pl.ds(pl.multiple_of(me_t * 8, 8), 8), :], trc1.at[me_t], t1r).start()
-
-    def local_solve(c):
-        def solve(kk, carry):
-            k = c * KC + kk
-            for m in range(V):
-                hi = xsplit[k, m * RL : m * RL + RL, 0:TL]
-                lo = xsplit[k, m * RL : m * RL + RL, TL : 2 * TL]
-                z = jnp.dot(jnp.concatenate([hi, lo], axis=0), gtab[k, m], preferred_element_type=F32)
-                z = z[0:RL, 0:TL] + z[RL : 2 * RL, 0:TL] + z[0:RL, TL : 2 * TL]
-                zbuf[m, pl.ds(pl.multiple_of(kk * RL, RL), RL), :] = z
-            return carry
-
-        lax.fori_loop(0, KC, solve, 0, unroll=4)
-
-        def out_mix(kk, carry):
-            rows = pl.ds(pl.multiple_of(kk * RL, RL), RL)
-            field = mix(1, c * KC + kk, jnp.concatenate([zbuf[n, rows, :] for n in range(V)], axis=0))
-            for m in range(V):
-                l2[m, pl.ds(pl.multiple_of((c * KC + kk) * RL, RL), RL), :] = field[m * RL : m * RL + RL]
-            return carry
-
-        lax.fori_loop(0, KC, out_mix, 0, unroll=4)
-
+    some_toeplitz(CUT_2, K)
     local_solve(0)
 
     u1, u2 = jnp.ones((8, TL), F32), jnp.ones((8, TL), F32)
@@ -427,38 +469,35 @@
     for d in range(nth):
         tx2[d] = jnp.where(forward, state[d], state[nth - 1 - d])
 
-    @pl.loop(1, nth)
+    @pl.loop(0, nth - 1)
     def _(i):
-        d = lax.rem(me_t + i, nth)
+        d = theta_peer(me_t, i, nth)
         pltpu.make_async_remote_copy(
             src_ref=tx2.at[d],
-            dst_ref=trc2.at[pl.ds(pl.multiple_of(me_t * 8, 8), 8), :],
+            dst_ref=infl.at[pl.ds(pl.multiple_of(me_t * 8, 8), 8), :],
             send_sem=t2s,
             recv_sem=t2r,
             device_id={"theta": d},
             device_id_type=MESH,
         ).start()
 
-    pltpu.make_async_copy(tx2.at[me_t], trc2.at[pl.ds(pl.multiple_of(me_t * 8, 8), 8), :], t2r).start()
+    pltpu.make_async_copy(tx2.at[me_t], infl.at[pl.ds(pl.multiple_of(me_t * 8, 8), 8), :], t2r).start()
 
     @pl.loop(1, nchunk)
     def _(c):
         local_solve(c)
 
-    pltpu.make_async_copy(trc2, trc2, t2r).wait()
-    final = pltpu.make_async_copy(trc2, infl, fin_sem)
-    final.start()
+    pltpu.make_async_copy(infl, infl, t2r).wait()
 
     @pl.loop(0, nchunk)
     def _(c):
-        sent = rcv1.at[c, pl.ds(0, nrow - 1)]
+        sent = rcv1.at[c, pl.ds(0, nrow - 1), pl.ds(0, USED), :]
         pltpu.make_async_copy(sent, sent, s1s.at[c]).wait()
         pltpu.make_async_copy(sent, sent, s2s.at[c]).wait()
 
     sent = trc1.at[pl.ds(0, nth - 1)]
     pltpu.make_async_copy(sent, sent, t1s).wait()
     pltpu.make_async_copy(sent, sent, t2s).wait()
-    final.wait()
 
 
 def finish_kernel(sizes, l2, infl, etab, gain, out, buf, sem):
@@ -475,11 +514,15 @@
     def _(j):
         state = infl[pl.ds(j, RL, stride=8), :]
         hi, lo = split(gain[j] * jnp.concatenate([state] * V, axis=0))
-        left = jnp.concatenate([hi, lo, hi], axis=1)
+        left = jnp.concatenate([hi, lo], axis=1)
         response = etab[pl.ds(pl.multiple_of(j * TL, TL), TL), :]
         for kk in range(tile):
             ehi, elo = split(jnp.where(row == kk, response, 0.0))
-            inflow = jnp.dot(left, jnp.concatenate([ehi, ehi, elo], axis=0), preferred_element_type=F32)
+            right = jnp.concatenate(
+                [jnp.concatenate([ehi, ehi], axis=0), jnp.concatenate([elo, jnp.zeros_like(elo)], axis=0)], axis=1
+            )
+            inflow = jnp.dot(left, right, preferred_element_type=F32)
+            inflow = inflow[:, 0:TL] + inflow[:, TL : 2 * TL]
             rows = pl.ds(pl.multiple_of(j * kr + kk * RL, RL), RL)
             for m in range(V):
                 buf[m, rows, :] = l2[m, rows, :] + inflow[m * RL : m * RL + RL]
@@ -522,11 +565,14 @@
             pltpu.VMEM((V, K, TL), F32),
             pltpu.VMEM((V, K, TL), F32),
             pltpu.VMEM((K * LINE, TL), F32),
-            pltpu.VMEM((nline, 3 * TL, TL), BF16),
+            pltpu.VMEM((nline, 2 * TL, 2 * TL), BF16),
             pltpu.VMEM((K, V, TL, 2 * TL), BF16),
-            pltpu.VMEM((2, V, K, 3 * TL), F32),
+            pltpu.VMEM((RL, V * V * K, TL), F32),
+            pltpu.VMEM((V, K, 3 * TL), F32),
+            pltpu.VMEM((K, V, 16, 3 * TL), BF16),
             pltpu.VMEM((V * K * 8, TL), F32),
             pltpu.VMEM((K, V * RL, 2 * TL), BF16),
+            pltpu.VMEM((nchunk, V, kr, TL), F32),
             pltpu.VMEM((nchunk, nrow * SLOT, TL), F32),
             pltpu.VMEM((nchunk, nrow, SLOT, TL), F32),
             pltpu.VMEM((nchunk, nrow, SLOT, TL), F32),
@@ -534,9 +580,8 @@
             pltpu.VMEM((RL * 8, TL), F32),
             pltpu.VMEM((nth, 8, TL), F32),
             pltpu.VMEM((nth, 8, TL), F32),
-            pltpu.VMEM((nth * 8, TL), F32),
             dma((nchunk,)), dma((nchunk,)), dma((nchunk,)), dma((nchunk,)), dma((nchunk,)),
-            dma, dma, dma, dma, dma,
+            dma, dma, dma, dma,
         ],
         compiler_params=pltpu.CompilerParams(
             collective_id=0, has_side_effects=True, vmem_limit_bytes=58 * 1024 * 1024

time: 49.1 us -> 43.4 us (0.88)
  Pallas kernels: 49 us -> 43.3 us
    pallas_call x1, Pallas kernels: 46 us -> 40.5 us  [body(): pl.pallas_call(functools.partial(solve_kernel, sizes), out_shape=(pltpu.V...]
where the time goes in v2:
time: 43.4 us; the launch traced here: 43.3 us
  Pallas kernels  43.3 us (100%)
    pallas_call x1, Pallas kernels, body(): pl.pallas_call(functools.partial(solve_kernel, sizes), out_shape=(pltpu.V...  40.5 us
    pallas_call x1, Pallas kernels, body(): pl.pallas_call(functools.partial(finish_kernel, sizes), out_shape=field,...  2.81 us

profile of v2, /device:TPU:1, one launch (start us, length us, event | category | flops | bytes accessed | tf_op | source)
XLA Modules:
  0.0 43.3 jit_solution(7862265952247463231)
XLA Ops:
  0.0 40.5 %solve.1 = (f32[5,1024,128]{2,1,0:T(8,128)S(1)}, f32[256,128]{1,0:T(8,128)S(1)}, f32[1024,128]{1,0:T(8,128)S(1)}, f32[8,160,128]{2,1,0:T(8,128)S(1)}) custom-call(f32[5,1024,128]{2,1,0:T(8,128)} %bitcast.6, f32[5,2,32]{2,1,0:T(2,128)} %bitcast.9, f32[5,2,32]{2,1,0:T(2,128)} %bitcast.10, f32[25,32,32]{2,1,0:T(8,128)} %bitcast.7, f32[25,32,32]{2,1,0:T(8,128)} %bitcast.8), custom_call_target="tpu_custom_call" | custom-call | tf_op jit(solution)/shard_map/solve/pallas_call | solution.py:548
  40.5 2.8 %finish.1 = f32[5,1024,128]{2,1,0:T(8,128)} custom-call(f32[5,1024,128]{2,1,0:T(8,128)S(1)} %get-tuple-element.9.l2, f32[256,128]{1,0:T(8,128)S(1)} %get-tuple-element.10.infl, f32[1024,128]{1,0:T(8,128)S(1)} %get-tuple-element.11.etab, f32[8,160,128]{2,1,0:T(8,128)S(1)} %get-tuple-element.12.gain), custom_call_target="tpu_custom_call" | custom-call | tf_op jit(solution)/shard_map/finish/pallas_call | solution.py:591

commit v3 on v2

--- a/solution.py
+++ b/solution.py
@@ -11,7 +11,7 @@
 KC = 8
 SLOT, USED = 24, 20
 STATES = 4
-CUT_1, CUT_2 = 0, 16
+CUT_2 = 12
 LINE = 32
 F32 = jnp.float32
 BF16 = jnp.bfloat16
@@ -250,19 +250,6 @@
         mcoef[2 * i] = both[:, 0:TL]
         mcoef[2 * i + 1] = both[:, TL : 2 * TL]
 
-    for m in range(V):
-        four = jnp.concatenate([mixo[m * V + n] for n in range(V - 1)], axis=1)
-        last = mixo[m * V + V - 1]
-        four_hi = four.astype(BF16).astype(F32)
-        last_hi = last.astype(BF16).astype(F32)
-        last = jnp.concatenate([last_hi, last_hi, last - last_hi, jnp.zeros_like(last)], axis=1)
-        mflat[m] = jnp.concatenate([four_hi, four - four_hi, last], axis=1)
-
-    @pl.loop(0, K)
-    def _(k):
-        for m in range(V):
-            mcat[k, m] = jnp.broadcast_to(mflat[m, pl.ds(k, 1), :], (16, 3 * TL)).astype(BF16)
-
     row16 = lax.broadcasted_iota(jnp.int32, (16, 3 * TL), 0)
     col16 = lax.broadcasted_iota(jnp.int32, (16, 3 * TL), 1) % RL
     on_diagonal = [jnp.where(row16 + 16 * half == col16, 1.0, 0.0).astype(BF16) for half in range(RL // 16)]
@@ -294,8 +281,6 @@
         @pl.loop(first, last)
         def _(k):
             toeplitz(k)
-
-    some_toeplitz(0, CUT_1)
 
     @pl.loop(0, nchunk)
     def _(c):
@@ -339,7 +324,7 @@
             o1.at[c, me_r, pl.ds(0, USED), :], rcv2.at[c, pl.ds(pl.multiple_of(me_r * SLOT, 8), USED), :], s2r.at[c]
         ).start()
 
-    some_toeplitz(CUT_1, CUT_2)
+    some_toeplitz(0, CUT_2)
 
     @pl.loop(0, nchunk)
     def _(c):
@@ -439,8 +424,20 @@
                 i = m * (K * 8 // TL) + j
                 gain[j * (TL // group) + q, m * RL : m * RL + RL, :] = spread_rows[i * RL : i * RL + RL]
 
+    for m in range(V):
+        four = jnp.concatenate([mixo[m * V + n] for n in range(V - 1)], axis=1)
+        last = mixo[m * V + V - 1]
+        four_hi = four.astype(BF16).astype(F32)
+        last_hi = last.astype(BF16).astype(F32)
+        last = jnp.concatenate([last_hi, last_hi, last - last_hi, jnp.zeros_like(last)], axis=1)
+        mflat[m] = jnp.concatenate([four_hi, four - four_hi, last], axis=1)
+
+    @pl.loop(0, K)
+    def _(k):
+        for m in range(V):
+            mcat[k, m] = jnp.broadcast_to(mflat[m, pl.ds(k, 1), :], (16, 3 * TL)).astype(BF16)
+
     some_toeplitz(CUT_2, K)
-    local_solve(0)
 
     u1, u2 = jnp.ones((8, TL), F32), jnp.ones((8, TL), F32)
     for kk in range(tile):
@@ -483,7 +480,7 @@
 
     pltpu.make_async_copy(tx2.at[me_t], infl.at[pl.ds(pl.multiple_of(me_t * 8, 8), 8), :], t2r).start()
 
-    @pl.loop(1, nchunk)
+    @pl.loop(0, nchunk)
     def _(c):
         local_solve(c)
 

time: 43.4 us -> 42.6 us (0.982)
  Pallas kernels: 43.3 us -> 42.5 us
    pallas_call x1, Pallas kernels: 40.5 us -> 39.7 us  [body(): pl.pallas_call(functools.partial(solve_kernel, sizes), out_shape=(pltpu.V...]
where the time goes in v3:
time: 42.6 us; the launch traced here: 42.5 us
  Pallas kernels  42.5 us (100%)
    pallas_call x1, Pallas kernels, body(): pl.pallas_call(functools.partial(solve_kernel, sizes), out_shape=(pltpu.V...  39.7 us
    pallas_call x1, Pallas kernels, body(): pl.pallas_call(functools.partial(finish_kernel, sizes), out_shape=field,...  2.81 us

profile of v3, /device:TPU:1, one launch (start us, length us, event | category | flops | bytes accessed | tf_op | source)
XLA Modules:
  0.0 42.5 jit_solution(17599332100888651110)
XLA Ops:
  0.0 39.7 %solve.1 = (f32[5,1024,128]{2,1,0:T(8,128)S(1)}, f32[256,128]{1,0:T(8,128)S(1)}, f32[1024,128]{1,0:T(8,128)S(1)}, f32[8,160,128]{2,1,0:T(8,128)S(1)}) custom-call(f32[5,1024,128]{2,1,0:T(8,128)} %bitcast.6, f32[5,2,32]{2,1,0:T(2,128)} %bitcast.9, f32[5,2,32]{2,1,0:T(2,128)} %bitcast.10, f32[25,32,32]{2,1,0:T(8,128)} %bitcast.7, f32[25,32,32]{2,1,0:T(8,128)} %bitcast.8), custom_call_target="tpu_custom_call" | custom-call | tf_op jit(solution)/shard_map/solve/pallas_call | solution.py:545
  39.7 2.8 %finish.1 = f32[5,1024,128]{2,1,0:T(8,128)} custom-call(f32[5,1024,128]{2,1,0:T(8,128)S(1)} %get-tuple-element.9.l2, f32[256,128]{1,0:T(8,128)S(1)} %get-tuple-element.10.infl, f32[1024,128]{1,0:T(8,128)S(1)} %get-tuple-element.11.etab, f32[8,160,128]{2,1,0:T(8,128)S(1)} %get-tuple-element.12.gain), custom_call_target="tpu_custom_call" | custom-call | tf_op jit(solution)/shard_map/finish/pallas_call | solution.py:588

commit v4 on v3

--- a/solution.py
+++ b/solution.py
@@ -232,13 +232,9 @@
     lax.fori_loop(0, V * nchunk, tables, 0, unroll=2)
 
     tile = TL // LINE
-    for j in range(K // tile):
-        hi, lo = split(wtab[j * TL : (j + 1) * TL, :].T)
-        wturn[j] = jnp.concatenate(
-            [jnp.concatenate([hi, hi], axis=0), jnp.concatenate([lo, jnp.zeros_like(lo)], axis=0)], axis=1
-        )
-
-    hi, lo = split(mixm.reshape(V * V * K, RL)[...])
+
+    scaled = [mixm[m * V + n] * rcoef[2, n][:, 0:RL] for m in range(V) for n in range(V)]
+    hi, lo = split(jnp.concatenate(scaled, axis=0))
     halves = jnp.concatenate([hi, lo], axis=1)
     pick_row = lax.broadcasted_iota(jnp.int32, (2 * RL, 2 * TL), 0) % RL
     pick_half = lax.broadcasted_iota(jnp.int32, (2 * RL, 2 * TL), 1) // TL
@@ -326,6 +322,12 @@
 
     some_toeplitz(0, CUT_2)
 
+    for j in range(K // tile):
+        hi, lo = split(wtab[j * TL : (j + 1) * TL, :].T)
+        wturn[j] = jnp.concatenate(
+            [jnp.concatenate([hi, hi], axis=0), jnp.concatenate([lo, jnp.zeros_like(lo)], axis=0)], axis=1
+        )
+
     @pl.loop(0, nchunk)
     def _(c):
         arrived = rcv2.at[c, pl.ds(0, nrow * USED), :]
@@ -333,10 +335,8 @@
         states = [
             tuple(rcv2[c, pl.ds(s * V + m, KC, stride=SLOT), :] for s in range(4)) for m in range(V)
         ]
-        f2 = [rcoef[2, m, pl.ds(c * KC, KC), :] for m in range(V)]
 
         def emit(r, z):
-            z = [f2[m] * z[m] for m in range(V)]
             for m in range(V):
                 total = None
                 for n in range(V):

time: 42.6 us -> 42.4 us (level)
  no operation moved by 1% of the time
where the time goes in v4:
time: 42.4 us; the launch traced here: 42.3 us
  Pallas kernels  42.3 us (100%)
    pallas_call x1, Pallas kernels, body(): pl.pallas_call(functools.partial(solve_kernel, sizes), out_shape=(pltpu.V...  39.5 us
    pallas_call x1, Pallas kernels, body(): pl.pallas_call(functools.partial(finish_kernel, sizes), out_shape=field,...  2.81 us

profile of v4, /device:TPU:1, one launch (start us, length us, event | category | flops | bytes accessed | tf_op | source)
XLA Modules:
  0.0 42.3 jit_solution(10231855687430502443)
XLA Ops:
  0.0 39.5 %solve.1 = (f32[5,1024,128]{2,1,0:T(8,128)S(1)}, f32[256,128]{1,0:T(8,128)S(1)}, f32[1024,128]{1,0:T(8,128)S(1)}, f32[8,160,128]{2,1,0:T(8,128)S(1)}) custom-call(f32[5,1024,128]{2,1,0:T(8,128)} %bitcast.6, f32[5,2,32]{2,1,0:T(2,128)} %bitcast.9, f32[5,2,32]{2,1,0:T(2,128)} %bitcast.10, f32[25,32,32]{2,1,0:T(8,128)} %bitcast.7, f32[25,32,32]{2,1,0:T(8,128)} %bitcast.8), custom_call_target="tpu_custom_call" | custom-call | tf_op jit(solution)/shard_map/solve/pallas_call | solution.py:545
  39.5 2.8 %finish.1 = f32[5,1024,128]{2,1,0:T(8,128)} custom-call(f32[5,1024,128]{2,1,0:T(8,128)S(1)} %get-tuple-element.9.l2, f32[256,128]{1,0:T(8,128)S(1)} %get-tuple-element.10.infl, f32[1024,128]{1,0:T(8,128)S(1)} %get-tuple-element.11.etab, f32[8,160,128]{2,1,0:T(8,128)S(1)} %get-tuple-element.12.gain), custom_call_target="tpu_custom_call" | custom-call | tf_op jit(solution)/shard_map/finish/pallas_call | solution.py:588
